TPU v7x, 128 devices: a whole 4x4x4 slice. The times are simulated.
128 devices in a mesh: ctx: 32 (over y_hi, x, z), head: 4 (over y_lo, core).
Axes of the slice: x: 4, y: 4 (y_hi: 2, y_lo: 2; y = y_hi * 2 + y_lo), z: 4, core: 2. Of those that a mesh axis runs over, the one named last changes fastest.
Arguments:
- queries: bfloat16 [32, 256, 8192], P('ctx', None, 'head'), may hold values from -64 to 64
- keys: bfloat16 [131072, 8, 128], P('ctx', 'head'), may hold values from -6 to 6
- values: bfloat16 [131072, 8, 128], P('ctx', 'head'), may hold values from -6 to 6
- lengths: int32 [32], P('ctx'), may hold values from 1024 to 4096, as said below
- owner: int32 [1], replicated, may hold values from 0 to 31
- w_out: bfloat16 [8192, 8192], P('head', 'ctx'), may hold values from -0.0625 to 0.0625
Outputs:
- attended: bfloat16 [256, 8192], P(None, 'head')
- projected: bfloat16 [256, 8192], P('head', 'ctx')
Inputs may be any that keep to these rules, and one draw needn't show every extreme that they name: `lengths`: some host's block is full.
All inputs are finite; a program needn't handle non-finite values.
Results may differ from a plain program's by a relative error of at most 0.015.
Values may be sent and summed in bfloat16 or wider, within the bound.
A program may use at most 256 MiB of HBM per device.

v0:
```python
import math

import jax
import jax.numpy as jnp
from jax import lax
from jax.sharding import PartitionSpec as P

KB = 512


NEGATIVE = -1e30


def spread(block, axis, holder):
    block = jnp.where(lax.axis_index(axis) == holder, block, jnp.zeros_like(block))
    return lax.psum(block, axis)


def combine_partials(first_part, second_part):
    peak_first, total_first, weighted_first = first_part
    peak_second, total_second, weighted_second = second_part
    peak = jnp.maximum(peak_first, peak_second)
    factor_first = jnp.exp(peak_first - peak)
    factor_second = jnp.exp(peak_second - peak)
    total = total_first * factor_first + total_second * factor_second
    weighted = weighted_first * factor_first[..., None] + weighted_second * factor_second[..., None]
    return (peak, total, weighted)


def finish_rows(total, weighted):
    normed = (weighted / total[..., None]).astype(jnp.bfloat16)
    return normed.transpose(2, 0, 1, 3).reshape(normed.shape[2], -1)


def body(queries, keys, values, lengths, owner, w_out):
    source = owner[0]
    received = spread(queries[0], "ctx", source)
    row_count = received.shape[0]
    kv_heads = keys.shape[1]
    head_width = keys.shape[2]
    per_group = received.shape[1] // (kv_heads * head_width)
    grouped = received.reshape(row_count, kv_heads, per_group, head_width)
    count = keys.shape[0] // KB
    key_blocks = keys.reshape(count, KB, kv_heads, head_width)
    value_blocks = values.reshape(count, KB, kv_heads, head_width)
    offsets = jnp.arange(count, dtype=jnp.int32) * KB
    valid_count = lengths[0]
    score_scale = 1.0 / math.sqrt(head_width)

    def absorb(running, element):
        key_block, value_block, offset = element
        usable = offset + jnp.arange(KB, dtype=jnp.int32) < valid_count
        scores = (
            jnp.einsum("rgjd,kgd->gjrk", grouped, key_block, preferred_element_type=jnp.float32)
            * score_scale
        )
        masked = jnp.where(usable, scores, NEGATIVE)
        peak = jnp.max(masked, axis=-1)
        weights = jnp.where(usable, jnp.exp(scores - peak[..., None]), 0.0).astype(jnp.bfloat16)
        total = jnp.sum(weights.astype(jnp.float32), axis=-1)
        weighted = jnp.einsum(
            "gjrk,kgd->gjrd", weights, value_block, preferred_element_type=jnp.float32
        )
        return (combine_partials(running, (peak, total, weighted)), None)

    start = (
        jnp.full((kv_heads, per_group, row_count), NEGATIVE, jnp.float32),
        jnp.zeros((kv_heads, per_group, row_count), jnp.float32),
        jnp.zeros((kv_heads, per_group, row_count, head_width), jnp.float32),
    )
    (peak, total, weighted), _ = lax.scan(absorb, start, (key_blocks, value_blocks, offsets))
    local = (weighted / total[..., None]).astype(jnp.bfloat16)
    log_sum = peak + jnp.log(total)
    top = lax.pmax(log_sum, "ctx")
    factor = jnp.exp(log_sum - top)
    numer, denom = lax.psum((local.astype(jnp.float32) * factor[..., None], factor), "ctx")
    attended = finish_rows(denom, numer)
    projected = lax.psum_scatter(
        jnp.dot(attended, w_out, preferred_element_type=jnp.float32),
        "head",
        scatter_dimension=0,
        tiled=True,
    ).astype(jnp.bfloat16)
    return (attended, projected)


def solution(mesh):
    in_specs = (
        P("ctx", None, "head"),
        P("ctx", "head", None),
        P("ctx", "head", None),
        P("ctx"),
        P(),
        P("head", "ctx"),
    )
    out_specs = (P(None, "head"), P("head", "ctx"))
    return jax.shard_map(body, mesh=mesh, in_specs=in_specs, out_specs=out_specs, check_vma=False)
```

profile of v0, /device:TPU:1, one launch (start us, length us, event | category | flops | bytes accessed | tf_op | source)
XLA Modules:
  0.0 1034.2 jit_solution(11373214518501982393)
XLA Ops:
  8.0 1.5 copy.12
  10.6 334.5 %all-reduce.3.cloned.1.call-done = bf16[256,2,8,128]{0,3,2,1:T(8,128)(2,1)} async-done(((bf16[256,2,8,128]{0,3,2,1:T(8,128)(2,1)}), bf16[256,2,8,128]{0,3,2,1:T(8,128)(2,1)}) %all-reduce.3.cloned.1.call-update) | async-done | bytes 1048592 | tf_op jit(solution)/shard_map/psum | solution.py:16
  345.1 1.6 copy.15
  346.8 96.4 %while.15 = (s32[]{:T(128)}, f32[2,8,256]{2,1,0:T(8,128)S(1)}, f32[2,8,256]{2,1,0:T(8,128)S(1)}, f32[2,8,256,128]{3,2,1,0:T(8,128)}, s32[8]{0:T(128)S(1)}, /*ind...) while((s32[]{:T(128)}, f32[2,8,256]{2,1,0:T(8,128)S(1)}, ...), condition=%wide.region_4.5_spmd.clone, body=%wide.region_1.4_spmd.clone.sunk | while | flops 1103127552 | bytes 48990412 | solution.py:71
  348.7 1.4 constant_dynamic-slice_fusion.3
  351.4 2.0 convert_reduce_fusion.2
  353.5 4.0 fusion.22
  360.7 1.4 constant_dynamic-slice_fusion.3
  363.5 2.0 convert_reduce_fusion.2
  365.5 4.0 fusion.22
  372.8 1.4 constant_dynamic-slice_fusion.3
  375.5 2.0 convert_reduce_fusion.2
  377.6 4.0 fusion.22
  384.8 1.4 constant_dynamic-slice_fusion.3
  387.6 2.0 convert_reduce_fusion.2
  389.6 4.0 fusion.22
  396.9 1.4 constant_dynamic-slice_fusion.3
  399.6 2.0 convert_reduce_fusion.2
  401.7 4.0 fusion.22
  411.7 2.0 convert_reduce_fusion.2
  413.7 4.0 fusion.22
  423.7 2.0 convert_reduce_fusion.2
  425.7 4.0 fusion.22
  435.8 2.0 convert_reduce_fusion.2
  437.8 4.0 fusion.22
  443.2 154.6 %pmax.7 = f32[2,8,256]{2,1,0:T(8,128)S(1)} all-reduce(f32[2,8,256]{2,1,0:T(8,128)S(1)} %log_add_fusion), channel_id=1, replica_groups=mesh['ctx'=32,'head'=4] {'ctx'}, use_global_device_ids=true, to_apply=%region_5.6 | all-reduce | flops 4096 | bytes 32768 | tf_op jit(solution)/shard_map/pmax | solution.py:74
  597.8 4.2 convert_multiply_fusion
  602.1 150.4 %psum.23 = f32[2,8,256]{2,1,0:T(8,128)S(1)} all-reduce(f32[2,8,256]{2,1,0:T(8,128)S(1)} %subtract_exponential_fusion.2), channel_id=1, replica_groups=mesh['ctx'=32,'head'=4] {'ctx'}, use_global_device_ids=true, to_apply=%region_7.8 | all-reduce | flops 4096 | bytes 32768 | tf_op jit(solution)/shard_map/psum | solution.py:76
  752.5 229.4 %all-reduce.5.cloned.1.call-done = f32[2,8,256,128]{3,2,1,0:T(8,128)} async-done(((f32[2,8,256,128]{3,2,1,0:T(8,128)}), f32[2,8,256,128]{3,2,1,0:T(8,128)}) %all-reduce.5.cloned.1.call-update) | async-done | bytes 2097168 | tf_op jit(solution)/shard_map/psum | solution.py:76
  981.9 1.9 fusion.8
  986.0 40.2 %reduce-scatter.2.cloned.1.call-done = f32[64,256]{1,0:T(8,128)} async-done(((f32[256,256]{1,0:T(8,128)}), f32[64,256]{1,0:T(8,128)}) %reduce-scatter.2.cloned.1.call-update) | async-done | bytes 65552 | tf_op jit(solution)/shard_map/reduce_scatter | solution.py:78
  1026.2 1.5 convert_element_type.21
  (87 shorter events, 44.3 us)
Async XLA Ops:
  7.2 977.7 %copy-start = (bf16[2048,256]{1,0:T(8,128)(2,1)S(1)}, bf16[2048,256]{1,0:T(8,128)(2,1)}, u32[]{:S(2)}) copy-start(bf16[2048,256]{1,0:T(8,128)(2,1)} %param.13) | copy-start | bytes 3145732
  7.2 338.0 %all-reduce.3.cloned.1.call-start = ((), (), s32[]{:S(2)}) async-start(), calls=%async_computation.1 | async-start | bytes 2097152 | tf_op jit(solution)/shard_map/psum | solution.py:16
  10.5 971.4 %all-reduce.5.cloned.1.call-start = ((), (), s32[]{:S(2)}) async-start(), calls=%async_computation.2 | async-start | bytes 4194304 | tf_op jit(solution)/shard_map/psum | solution.py:76
  351.4 2.0 copy-start.2
  357.5 1.4 copy-start.3
  363.5 2.0 copy-start.2
  369.5 1.4 copy-start.3
  375.5 2.0 copy-start.2
  381.6 1.4 copy-start.3
  387.6 2.0 copy-start.2
  393.6 1.4 copy-start.3
  399.6 2.0 copy-start.2
  405.7 1.4 copy-start.3
  411.7 2.0 copy-start.2
  417.7 1.4 copy-start.3
  423.7 2.0 copy-start.2
  429.8 1.4 copy-start.3
  435.8 2.0 copy-start.2
  441.8 1.4 copy-start.3
  602.1 424.1 %reduce-scatter.2.cloned.1.call-start = ((), (), s32[]{:S(2)}) async-start(), calls=%async_computation.3 | async-start | bytes 327680 | tf_op jit(solution)/shard_map/reduce_scatter | solution.py:78
  984.8 42.8 %copy-start.1 = (bf16[32,8,16,128]{3,1,2,0:T(8,128)(2,1)}, bf16[32,8,16,128]{3,1,2,0:T(8,128)(2,1)S(1)}, u32[]{:S(2)}) copy-start(bf16[32,8,16,128]{3,1,2,0:T(8,128)(2,1)S(1)} %copy.35) | copy-start | bytes 3145732
Sparse Core Ops, SparseCore 0:
  11.1 334.0 all-reduce.2
  602.2 379.6 all-reduce.4
  986.1 39.9 reduce-scatter.1
where the time goes:
time: 1030 us
  waiting for transfers between devices  604 us (59%)
  blocking collectives  305 us (30%)
  matrix products  44 us (4%)
  other arithmetic  35.1 us (3%)
  local copies, waits for them, and re-layouts  30.7 us (3%)
  between operations  14.6 us (1%)
    psum x1, waiting for transfers between devices, spread(): return lax.psum(block, axis)  335 us
    psum x1, waiting for transfers between devices, body(): lax.psum((local.astype(jnp.float32) * factor[..., None], factor), 'ctx')  229 us
    pmax x1, blocking collectives, body(): top = lax.pmax(log_sum, 'ctx')  155 us
    psum x1, blocking collectives, body(): lax.psum((local.astype(jnp.float32) * factor[..., None], factor), 'ctx')  150 us
    reduce_scatter x1, waiting for transfers between devices, body(): lax.psum_scatter(jnp.dot(attended, w_out, preferred_element_type=jnp.floa...  40.2 us
    dot_general x8, matrix products, absorb(): jnp.einsum('gjrk,kgd->gjrd', weights, value_block, preferred_element_type...  32.1 us
  transfers between devices with their start and end apart: 3, of which 3 were waited for; matrix products, arithmetic and copies ran while one was open for 0% of the time, Pallas kernels for 0%

commit v1 on v0

v1 whole, which is shorter than its diff:
```python
import functools
import math

import jax
import jax.numpy as jnp
from jax import lax
from jax.experimental import pallas as pl
from jax.experimental.pallas import tpu as pltpu
from jax.sharding import PartitionSpec as P

MESH = pl.DeviceIdType.MESH
HOSTS = 32
GROUPS = 8
ROWS = 256
HD = 128
KEYS = 4096
CHUNK = 1024
SCALE = math.log2(math.e) / math.sqrt(HD)
QB = 4
LAG = 2


def remote(src, dst, send, recv, ctx):
    return pltpu.make_async_remote_copy(
        src_ref=src, dst_ref=dst, send_sem=send, recv_sem=recv, device_id=ctx, device_id_type=MESH
    )


def drain(ref, sem):
    pltpu.make_async_copy(ref, ref, sem).wait()


def scatter_kernel(owner, q_ref, out_ref, send, recv):
    me = lax.axis_index("ctx")
    barrier = pltpu.get_barrier_semaphore()

    @pl.when(me != owner)
    def _():
        pl.semaphore_signal(barrier, inc=1, device_id={"ctx": owner}, device_id_type=MESH)
        drain(out_ref, recv)

    @pl.when(me == owner)
    def _():
        pl.semaphore_wait(barrier, HOSTS - 1)

        def piece(p):
            return q_ref.at[0, pl.ds(16 * (p % 16), 16), pl.ds(1024 * (p // 16), 1024)]

        copies = []
        for step in range(1, HOSTS):
            p = (owner + step) % HOSTS
            copies.append(remote(piece(p), out_ref, send.at[step], recv, {"ctx": p}))
            copies[-1].start()
        own = pltpu.make_async_copy(piece(owner), out_ref, send.at[0])
        own.start()
        own.wait()
        for copy in copies:
            copy.wait_send()


def scatter(owner, queries):
    return pl.pallas_call(
        functools.partial(scatter_kernel, owner),
        out_shape=jax.ShapeDtypeStruct((16, 1024), jnp.bfloat16),
        in_specs=[pl.BlockSpec(memory_space=pl.ANY)],
        out_specs=pl.BlockSpec(memory_space=pltpu.VMEM),
        scratch_shapes=[pltpu.SemaphoreType.DMA((HOSTS,)), pltpu.SemaphoreType.DMA],
        compiler_params=pltpu.CompilerParams(collective_id=owner + 1, has_side_effects=True),
    )(queries)


def main_kernel(
    qp_ref, k_hbm, v_hbm, len_ref, w_hbm, att_hbm, proj_ref,
    k_in, v_in, w_ref, k_ref, vt_ref, q_ref, sa, sb, o_buf, o_recv, l_buf, l_recv, at_piece, at_buf,
    part, hd_buf, hd_recv, local_sem, q_send, q_recv, o_send, o_rsem, l_send, l_rsem, a_send, a_recv, h_send, h_rsem,
):
    me = lax.axis_index("ctx")
    hd = lax.axis_index("head")
    my_kv, my_row = me // 16, lax.rem(me, 16)
    loads = [
        pltpu.make_async_copy(k_hbm, k_in, local_sem.at[0]),
        pltpu.make_async_copy(v_hbm, v_in, local_sem.at[1]),
        pltpu.make_async_copy(w_hbm, w_ref, local_sem.at[2]),
    ]
    for load in loads:
        load.start()
    barrier = pltpu.get_barrier_semaphore()

    def greet(i, _):
        pl.semaphore_signal(barrier, inc=1, device_id={"ctx": lax.rem(me + i, HOSTS)}, device_id_type=MESH)
        return _

    lax.fori_loop(1, HOSTS, greet, 0)
    for i in (1, 2, 3):
        pl.semaphore_signal(barrier, inc=1, device_id={"head": lax.rem(hd + i, 4)}, device_id_type=MESH)
    pl.semaphore_wait(barrier, HOSTS - 1 + 3)

    width = 1024 // QB
    for b in range(QB):
        cols = pl.ds(b * width, width)
        src = qp_ref.at[:, cols]
        dst = q_ref.at[my_kv, pl.ds(pl.multiple_of(16 * my_row, 16), 16), cols]

        def send_q(i, _):
            remote(src, dst, q_send.at[b], q_recv.at[b], {"ctx": lax.rem(me + i, HOSTS)}).start()
            return _

        lax.fori_loop(1, HOSTS, send_q, 0)
        pltpu.make_async_copy(src, dst, q_recv.at[b]).start()

    count = len_ref[0]
    loads[0].wait()
    for g in range(2):
        first = k_in[0:1, g, :]

        def prep_k(c, _):
            at = pl.multiple_of(c * 512, 512)
            row = lax.broadcasted_iota(jnp.int32, (512, HD), 0) + at
            k_ref[g, pl.ds(at, 512), :] = jnp.where(row < count, k_in[pl.ds(at, 512), g, :], first)
            return _

        lax.fori_loop(0, KEYS // 512, prep_k, 0)
    loads[1].wait()
    for g in range(2):

        def prep_v(c, _):
            at = pl.multiple_of(c * 512, 512)
            row = lax.broadcasted_iota(jnp.int32, (512, HD), 0) + at
            v = jnp.where(row < count, v_in[pl.ds(at, 512), g, :].astype(jnp.float32), 0.0)
            vt_ref[g, 0:HD, pl.ds(at, 512)] = v.T.astype(jnp.bfloat16)
            col = lax.broadcasted_iota(jnp.int32, (16, 512), 1) + at
            vt_ref[g, HD : HD + 16, pl.ds(at, 512)] = jnp.where(col < count, 1.0, 0.0).astype(jnp.bfloat16)
            return _

        lax.fori_loop(0, KEYS // 512, prep_v, 0)

    def head_q(g, kv):
        return q_ref[kv, :, pl.ds(pl.multiple_of(g * HD, HD), HD)]

    def scores(kv, c, q, s_ref, top):
        at = c * CHUNK
        s = lax.dot_general(
            k_ref[kv, at : at + CHUNK, :], q, (((1,), (1,)), ((), ())), preferred_element_type=jnp.float32
        )
        s_ref[at : at + CHUNK, :] = s
        return jnp.maximum(top, jnp.max(s.reshape(CHUNK // 8, 8, ROWS), axis=0))

    def weigh(kv, c, s_ref, top, acc):
        at = c * CHUNK
        p = jnp.exp2(s_ref[at : at + CHUNK, :] * SCALE - top).astype(jnp.bfloat16)
        return acc + jnp.dot(vt_ref[kv, 0 : HD + 8, at : at + CHUNK], p, preferred_element_type=jnp.float32)

    def finish(g, kv, acc, top):
        total = acc[HD : HD + 1]
        o_buf[g, kv] = (acc[:HD] / total).T.astype(jnp.bfloat16)
        lse = top + jnp.log2(total)
        l_buf[g, kv, 0] = lse[:, :128]
        l_buf[g, kv, 1] = lse[:, 128:]

    low = jnp.full((8, ROWS), -jnp.inf, jnp.float32)
    zero = jnp.zeros((HD + 8, ROWS), jnp.float32)

    def attend(g, best):
        top = jnp.max(best, axis=0, keepdims=True) * SCALE
        q = head_q(g, 1)
        other, acc = low, zero
        for c in range(KEYS // CHUNK):
            other = scores(1, c, q, sb, other)
            acc = weigh(0, c, sa, top, acc)
        finish(g, 0, acc, top)
        top = jnp.max(other, axis=0, keepdims=True) * SCALE
        q = head_q(jnp.minimum(g + 1, GROUPS - 1), 0)
        best, acc = low, zero
        for c in range(KEYS // CHUNK):
            best = scores(0, c, q, sa, best)
            acc = weigh(1, c, sb, top, acc)
        finish(g, 1, acc, top)
        return best

    def send_out(g):
        def one(i, _):
            p = lax.rem(me + i, HOSTS)
            kv, row = p // 16, lax.rem(p, 16)
            remote(
                o_buf.at[g, kv, pl.ds(pl.multiple_of(16 * row, 16), 16), :], o_recv.at[g, me],
                o_send.at[g], o_rsem.at[g], {"ctx": p},
            ).start()
            remote(l_buf.at[g, kv, row // 8], l_recv.at[g, me], l_send.at[g], l_rsem.at[g], {"ctx": p}).start()
            return _

        lax.fori_loop(1, HOSTS, one, 0)
        pltpu.make_async_copy(
            o_buf.at[g, my_kv, pl.ds(pl.multiple_of(16 * my_row, 16), 16), :], o_recv.at[g, me], o_rsem.at[g]
        ).start()
        pltpu.make_async_copy(l_buf.at[g, my_kv, my_row // 8], l_recv.at[g, me], l_rsem.at[g]).start()

    def combine(g):
        drain(l_recv.at[g], l_rsem.at[g])
        drain(o_recv.at[g], o_rsem.at[g])
        lse = l_recv[g, :, 0, :]
        w = jnp.exp2(lse - jnp.max(lse, axis=0, keepdims=True))
        w = w / jnp.sum(w, axis=0, keepdims=True)
        w = pltpu.roll(w, lax.rem(128 - 16 * lax.rem(my_row, 8), 128), 1)
        w = jnp.concatenate([w, jnp.zeros((96, 128), jnp.float32)], 0).T[:16]
        acc = jnp.zeros((16, HD), jnp.float32)
        for h in range(HOSTS):
            acc = acc + w[:, h : h + 1] * o_recv[g, h].astype(jnp.float32)
        at_piece[g] = acc.astype(jnp.bfloat16)
        cols = pl.ds(pl.multiple_of(g * HD, HD), HD)
        dst = at_buf.at[my_kv, pl.ds(pl.multiple_of(16 * my_row, 16), 16), cols]

        def one(i, _):
            remote(at_piece.at[g], dst, a_send.at[g], a_recv.at[g], {"ctx": lax.rem(me + i, HOSTS)}).start()
            return _

        lax.fori_loop(1, HOSTS, one, 0)
        pltpu.make_async_copy(at_piece.at[g], dst, a_recv.at[g]).start()

    def project(g):
        cols = pl.ds(pl.multiple_of(g * HD, HD), HD)
        drain(at_buf.at[:, :, cols], a_recv.at[g])
        for kv in range(2):
            rows = pl.ds(pl.multiple_of(kv * 1024 + g * HD, HD), HD)
            part[...] += jnp.dot(at_buf[kv, :, cols], w_ref[rows, :], preferred_element_type=jnp.float32)

    part[...] = jnp.zeros_like(part)

    drain(q_ref.at[:, :, pl.ds(0, width)], q_recv.at[0])
    q = head_q(0, 0)
    best = low
    for c in range(KEYS // CHUNK):
        best = scores(0, c, q, sa, best)
    loads[2].wait()

    def step(g, best):
        for b in range(1, QB):
            @pl.when(g == 2 * b - 1)
            def _():
                drain(q_ref.at[:, :, pl.ds(b * width, width)], q_recv.at[b])

        best = attend(g, best)
        send_out(g)

        @pl.when(g >= LAG)
        def _():
            combine(g - LAG)

        @pl.when(g >= 2 * LAG)
        def _():
            project(g - 2 * LAG)

        return best

    lax.fori_loop(0, GROUPS, step, best)
    for g in range(GROUPS - LAG, GROUPS):
        combine(g)
    for g in range(GROUPS - 2 * LAG, GROUPS):
        project(g)

    outs = [
        pltpu.make_async_copy(at_buf.at[kv], att_hbm.at[:, pl.ds(kv * 1024, 1024)], local_sem.at[3 + kv])
        for kv in range(2)
    ]
    for out in outs:
        out.start()
    hd_buf[...] = part[...].astype(jnp.bfloat16)
    copies = []
    for i in (1, 2, 3):
        to = lax.rem(hd + i, 4)
        copies.append(
            remote(
                hd_buf.at[pl.ds(pl.multiple_of(64 * to, 64), 64), :], hd_recv.at[i - 1],
                h_send.at[i - 1], h_rsem.at[i - 1], {"head": to},
            )
        )
        copies[-1].start()
    total = part[pl.ds(pl.multiple_of(64 * hd, 64), 64), :]
    for i in range(3):
        copies[i].wait()
        total = total + hd_recv[i].astype(jnp.float32)
    proj_ref[...] = total.astype(jnp.bfloat16)

    for out in outs:
        out.wait()
    for b in range(QB):
        drain(o_recv.at[pl.ds(0, 1024 // QB // HD), pl.ds(0, HOSTS - 1)], q_send.at[b])
    for g in range(GROUPS):
        drain(o_recv.at[g, pl.ds(0, HOSTS - 1)], o_send.at[g])
        drain(l_recv.at[g, pl.ds(0, HOSTS - 1)], l_send.at[g])
        drain(o_recv.at[g, pl.ds(0, HOSTS - 1)], a_send.at[g])


def attention(qp, keys, values, lengths, w_out):
    vmem = pl.BlockSpec(memory_space=pltpu.VMEM)
    anywhere = pl.BlockSpec(memory_space=pl.ANY)
    bf, f32 = jnp.bfloat16, jnp.float32
    dma = pltpu.SemaphoreType.DMA
    return pl.pallas_call(
        main_kernel,
        out_shape=(jax.ShapeDtypeStruct((ROWS, 2048), bf), jax.ShapeDtypeStruct((64, 256), bf)),
        in_specs=[vmem, anywhere, anywhere, pl.BlockSpec(memory_space=pltpu.SMEM), anywhere],
        out_specs=(anywhere, vmem),
        scratch_shapes=[
            pltpu.VMEM((KEYS, 2, HD), bf), pltpu.VMEM((KEYS, 2, HD), bf), pltpu.VMEM((2048, 256), bf),
            pltpu.VMEM((2, KEYS, HD), bf), pltpu.VMEM((2, HD + 16, KEYS), bf),
            pltpu.VMEM((2, ROWS, 1024), bf),
            pltpu.VMEM((KEYS, ROWS), f32), pltpu.VMEM((KEYS, ROWS), f32),
            pltpu.VMEM((GROUPS, 2, ROWS, HD), bf), pltpu.VMEM((GROUPS, HOSTS, 16, HD), bf),
            pltpu.VMEM((GROUPS, 2, 2, 1, 128), f32), pltpu.VMEM((GROUPS, HOSTS, 1, 128), f32),
            pltpu.VMEM((GROUPS, 16, HD), bf), pltpu.VMEM((2, ROWS, 1024), bf),
            pltpu.VMEM((ROWS, 256), f32), pltpu.VMEM((ROWS, 256), bf), pltpu.VMEM((3, 64, 256), bf),
            dma((5,)), dma((QB,)), dma((QB,)), dma((GROUPS,)), dma((GROUPS,)), dma((GROUPS,)), dma((GROUPS,)),
            dma((GROUPS,)), dma((GROUPS,)), dma((3,)), dma((3,)),
        ],
        compiler_params=pltpu.CompilerParams(
            collective_id=0, has_side_effects=True, vmem_limit_bytes=56 << 20
        ),
    )(qp, keys, values, lengths, w_out)


def body(queries, keys, values, lengths, owner, w_out):
    qp = lax.switch(owner[0], [functools.partial(scatter, o) for o in range(HOSTS)], queries)
    return attention(qp, keys, values, lengths, w_out)


def solution(mesh):
    in_specs = (
        P("ctx", None, "head"),
        P("ctx", "head", None),
        P("ctx", "head", None),
        P("ctx"),
        P(),
        P("head", "ctx"),
    )
    out_specs = (P(None, "head"), P("head", "ctx"))
    return jax.shard_map(body, mesh=mesh, in_specs=in_specs, out_specs=out_specs, check_vma=False)
```

time: 1030 us -> 103 us (0.10)
  waiting for transfers between devices: 604 us -> 0 us
  blocking collectives: 305 us -> 0 us
  Pallas kernels: 0 us -> 98.1 us
  matrix products: 44 us -> 0 us
  other arithmetic: 35.1 us -> 0 us
  local copies, waits for them, and re-layouts: 30.7 us -> 2.93 us
  between operations: 14.6 us -> 1.95 us
    psum x2 -> x0, waiting for transfers between devices: 564 us -> none  [the longest x1 335 us: spread(): return lax.psum(block, axis)]
    pmax x1 -> x0, blocking collectives: 155 us -> none  [body(): top = lax.pmax(log_sum, 'ctx')]
    psum x1 -> x0, blocking collectives: 150 us -> none  [body(): lax.psum((local.astype(jnp.float32) * factor[..., None], factor), 'ctx')]
    pallas_call x0 -> x2, Pallas kernels: none -> 98.1 us  [the longest x1 85 us: attention(): pl.pallas_call(main_kernel, out_shape=(jax.ShapeDtypeStruct((ROWS, 2048),...]
    dot_general x17 -> x0, matrix products: 44 us -> none  [the longest x8 32.1 us: absorb(): jnp.einsum('gjrk,kgd->gjrd', weights, value_block, preferred_element_type...]
    reduce_scatter x1 -> x0, waiting for transfers between devices: 40.2 us -> none  [body(): lax.psum_scatter(jnp.dot(attended, w_out, preferred_element_type=jnp.floa...]
    dynamic_slice x16 -> x0, local copies, waits for them, and re-layouts: 15.8 us -> none  [body(): lax.scan(absorb, start, (key_blocks, value_blocks, offsets))]
    reduce_sum x8 -> x0, other arithmetic: 15.8 us -> none  [absorb(): total = jnp.sum(weights.astype(jnp.float32), axis=-1)]
  transfers between devices with their start and end apart: 3 -> 0, of which waited for: 3 -> 0; matrix products, arithmetic and copies ran while one was open for 0% -> 0% of each run, Pallas kernels for 0% -> 0%
where the time goes in v1:
time: 103 us
  Pallas kernels  98.1 us (95%)
  local copies, waits for them, and re-layouts  2.93 us (3%)
  between operations  1.95 us (2%)
    pallas_call x1, Pallas kernels, attention(): pl.pallas_call(main_kernel, out_shape=(jax.ShapeDtypeStruct((ROWS, 2048),...  85 us
    pallas_call x1, Pallas kernels, scatter(): pl.pallas_call(functools.partial(scatter_kernel, owner), out_shape=jax.Sh...  13.1 us
    unnamed x4, local copies, waits for them, and re-layouts  2.93 us

profile of v1, /device:TPU:1, one launch (start us, length us, event | category | flops | bytes accessed | tf_op | source)
XLA Modules:
  0.0 103.2 jit_solution(5061018219291676080)
XLA Ops:
  1.9 13.4 %conditional.1 = (bf16[16,1024]{1,0:T(8,128)(2,1)S(1)}) conditional(s32[]{:T(128)} %bitcast, bf16[1,256,2048]{2,1,0:T(8,128)(2,1)} %param.38, bf16[1,256,2048]{2,1,0:T(8,128)(2,1)} %param.38, bf16[1,256,2048]{2,1,0:T(8,128)(2,1)} %param.38, bf16[1,256,2048]{2,1,0:T(8,128)(2,1)} %param.38, ...), branch_computations={%region_0.0_spmd, %region_1.0_spmd, %region_2.0_spmd, %region_3.0_... | conditional | bytes 8 | solution.py:322
  2.0 13.1 %branch_2_fun.1 = bf16[16,1024]{1,0:T(8,128)(2,1)S(1)} custom-call(bf16[1,256,2048]{2,1,0:T(8,128)(2,1)} %q_ref.2), custom_call_target="tpu_custom_call" | custom-call | tf_op jit(solution)/shard_map/cond/branch_2_fun/pallas_call | solution.py:62
  15.3 85.0 %shard_map.173 = (bf16[256,2048]{1,0:T(8,128)(2,1)}, bf16[64,256]{1,0:T(8,128)(2,1)}) custom-call(bf16[16,1024]{1,0:T(8,128)(2,1)S(1)} %get-tuple-element.71.qp_ref, bf16[4096,2,128]{2,1,0:T(2,128)(2,1)} %k_hbm.1, bf16[4096,2,128]{2,1,0:T(2,128)(2,1)} %v_hbm.1, s32[1]{0:T(128)S(6)} %copy.42.len_ref, bf16[2048,256]{1,0:T(8,128)(2,1)} %w_hbm.1), custom_call_target="tpu_custom_call" | custom-call | tf_op jit(solution)/shard_map/pallas_call | solution.py:298
  100.3 0.0 copy-start
  100.3 2.3 %copy.44 = bf16[256,2048]{1,0:T(8,128)(2,1)} copy(bf16[256,2048]{1,0:T(8,128)(2,1)} %get-tuple-element.69) | data formatting | bytes 2097152
  102.6 0.0 copy-done
  102.6 0.6 copy.45
Async XLA Ops:
  100.3 2.3 %copy-start = (bf16[64,256]{1,0:T(8,128)(2,1)S(1)}, bf16[64,256]{1,0:T(8,128)(2,1)}, u32[]{:S(2)}) copy-start(bf16[64,256]{1,0:T(8,128)(2,1)} %get-tuple-element.70) | copy-start | bytes 98308

commit v2 on v1

v2 whole, which is shorter than its diff:
```python
import functools
import math

import jax
import jax.numpy as jnp
from jax import lax
from jax.experimental import pallas as pl
from jax.experimental.pallas import tpu as pltpu
from jax.sharding import PartitionSpec as P

MESH = pl.DeviceIdType.MESH
HOSTS = 32
GROUPS = 8
ROWS = 256
HD = 128
KEYS = 4096
CHUNK = 1024
SCALE = math.log2(math.e) / math.sqrt(HD)
STAGED = 4
AFTER = (0, 2, 4, 6, 8)
QUARTERS = tuple((yy, pl.ds(aa, 2)) for yy in range(2) for aa in (0, 2))
Q_BATCHES = ((0, 2, False), (2, 5, False), (5, 8, True))


def remote(src, dst, send, recv, ctx):
    return pltpu.make_async_remote_copy(
        src_ref=src, dst_ref=dst, send_sem=send, recv_sem=recv, device_id=ctx, device_id_type=MESH
    )


def drain(ref, sem):
    pltpu.make_async_copy(ref, ref, sem).wait()


def scatter_kernel(owner, q_ref, out_ref, send, recv):
    me = lax.axis_index("ctx")
    barrier = pltpu.get_barrier_semaphore()

    @pl.when(me != owner)
    def _():
        pl.semaphore_signal(barrier, inc=1, device_id={"ctx": owner}, device_id_type=MESH)
        drain(out_ref, recv)

    @pl.when(me == owner)
    def _():
        pl.semaphore_wait(barrier, HOSTS - 1)

        def piece(p):
            return q_ref.at[0, pl.ds(16 * (p % 16), 16), pl.ds(1024 * (p // 16), 1024)]

        copies = []
        for step in range(1, HOSTS):
            p = (owner + step) % HOSTS
            copies.append(remote(piece(p), out_ref, send.at[step], recv, {"ctx": p}))
            copies[-1].start()
        own = pltpu.make_async_copy(piece(owner), out_ref, send.at[0])
        own.start()
        own.wait()
        for copy in copies:
            copy.wait_send()


def scatter(owner, queries):
    return pl.pallas_call(
        functools.partial(scatter_kernel, owner),
        out_shape=jax.ShapeDtypeStruct((16, 1024), jnp.bfloat16),
        in_specs=[pl.BlockSpec(memory_space=pl.ANY)],
        out_specs=pl.BlockSpec(memory_space=pltpu.VMEM),
        scratch_shapes=[pltpu.SemaphoreType.DMA((HOSTS,)), pltpu.SemaphoreType.DMA],
        compiler_params=pltpu.CompilerParams(collective_id=owner + 1, has_side_effects=True),
    )(queries)


def main_kernel(
    qp_ref, k_hbm, v_hbm, len_ref, w_hbm, att_hbm, proj_ref,
    k_in, v_in, k_wide, v_wide, eye, w_ref, k_ref, vt_ref, q_ref, sa, sb,
    o_buf, l_buf, r1, l1, s2, l2_buf, r2, l2, d_recv, dl_recv, at_buf, w1, w2, part, hd_buf, hd_recv,
    local_sem, out_sem, q1_send, q1_recv, q2_send, q2_recv, o1_send, o1_recv, l1_send, l1_recv,
    o2_send, o2_recv, l2_send, l2_recv, a1_send, a1_recv, a2_send, a2_recv, h_send, h_recv,
):
    me = lax.axis_index("ctx")
    hd = lax.axis_index("head")
    y, x, z = me // 16, lax.rem(me // 4, 4), lax.rem(me, 4)
    loads = [
        pltpu.make_async_copy(k_hbm, k_in, local_sem.at[0]),
        pltpu.make_async_copy(v_hbm, v_in, local_sem.at[1]),
        pltpu.make_async_copy(w_hbm, w_ref, local_sem.at[2]),
    ]
    for load in loads:
        load.start()
    barrier = pltpu.get_barrier_semaphore()
    for i in range(1, HOSTS):
        pl.semaphore_signal(barrier, inc=1, device_id={"ctx": lax.rem(me + i, HOSTS)}, device_id_type=MESH)
    for i in range(1, 4):
        pl.semaphore_signal(barrier, inc=1, device_id={"head": lax.rem(hd + i, 4)}, device_id_type=MESH)
    pl.semaphore_wait(barrier, HOSTS - 1 + 3)

    def q_cols(b):
        first, last, _ = Q_BATCHES[b]
        return pl.ds(first * HD, (last - first) * HD)

    def q_plane(b):
        cols = q_cols(b)
        return q_ref.at[:, x, :, :, cols] if Q_BATCHES[b][2] else q_ref.at[:, :, z, :, cols]

    for b in range(len(Q_BATCHES)):
        src, dst = qp_ref.at[:, q_cols(b)], q_ref.at[y, x, z, :, q_cols(b)]
        if b == 0:
            for i in range(1, HOSTS):
                remote(src, dst, q1_send.at[b], q1_recv.at[b], {"ctx": lax.rem(me + i, HOSTS)}).start()
        for i in range(1, 8) if b else ():
            if Q_BATCHES[b][2]:
                q = lax.rem(4 * y + z + i, 8)
                to = 16 * (q // 4) + 4 * x + lax.rem(q, 4)
            else:
                q = lax.rem(4 * y + x + i, 8)
                to = 16 * (q // 4) + 4 * lax.rem(q, 4) + z
            remote(src, dst, q1_send.at[b], q1_recv.at[b], {"ctx": to}).start()
        pltpu.make_async_copy(src, dst, q1_recv.at[b]).start()

    def q_ring(b):
        drain(q_plane(b), q1_recv.at[b])
        for i in range(1, 4):
            to = 16 * y + 4 * lax.rem(x + i, 4) + z if Q_BATCHES[b][2] else 16 * y + 4 * x + lax.rem(z + i, 4)
            part_of = q_plane(b)
            for yy, at in QUARTERS:
                own = part_of.at[yy, at]
                remote(own, own, q2_send.at[b], q2_recv.at[b], {"ctx": to}).start()

    def q_ready(b):
        drain(q_ref.at[:, pl.ds(0, 3), :, :, q_cols(b)], q2_recv.at[b])

    count = len_ref[0]
    loads[0].wait()
    for c in range(KEYS // 512):
        at = 512 * c
        k_wide[2 * at : 2 * at + 1024, :] = k_in[2 * at : 2 * at + 1024, :].astype(jnp.float32)
        row = lax.broadcasted_iota(jnp.int32, (512, HD), 0) + at
        for kv in range(2):
            k_ref[kv, at : at + 512, :] = jnp.where(
                row < count, k_wide[pl.ds(2 * at + kv, 512, stride=2), :], k_wide[kv : kv + 1, :]
            ).astype(jnp.bfloat16)
    loads[1].wait()
    eye[...] = jnp.where(
        lax.broadcasted_iota(jnp.int32, (HD, HD), 0) == lax.broadcasted_iota(jnp.int32, (HD, HD), 1), 1.0, 0.0
    ).astype(jnp.bfloat16)
    for c in range(KEYS // 512):
        at = 512 * c
        v_wide[2 * at : 2 * at + 1024, :] = v_in[2 * at : 2 * at + 1024, :].astype(jnp.float32)
        row = lax.broadcasted_iota(jnp.int32, (512, HD), 0) + at
        col = lax.broadcasted_iota(jnp.int32, (16, 512), 1) + at
        for kv in range(2):
            v = jnp.where(row < count, v_wide[pl.ds(2 * at + kv, 512, stride=2), :], 0.0).astype(jnp.bfloat16)
            vt_ref[kv, 0:HD, at : at + 512] = lax.dot_general(
                eye[...], v, (((1,), (1,)), ((), ())), preferred_element_type=jnp.float32
            ).astype(jnp.bfloat16)
            vt_ref[kv, HD : HD + 16, at : at + 512] = jnp.where(col < count, 1.0, 0.0).astype(jnp.bfloat16)
    for b in range(1, len(Q_BATCHES)):
        q_ring(b)

    def head_q(g, kv):
        return q_ref[kv, :, :, :, pl.ds(pl.multiple_of(g * HD, HD), HD)].reshape(ROWS, HD)

    def scores(kv, c, q, s_ref, top):
        at = c * CHUNK
        s = lax.dot_general(
            k_ref[kv, at : at + CHUNK, :], q, (((1,), (1,)), ((), ())), preferred_element_type=jnp.float32
        )
        s_ref[at : at + CHUNK, :] = s
        return jnp.maximum(top, jnp.max(s.reshape(CHUNK // 8, 8, ROWS), axis=0))

    def weigh(kv, c, s_ref, top, acc):
        at = c * CHUNK
        p = jnp.exp2(s_ref[at : at + CHUNK, :] * SCALE - top).astype(jnp.bfloat16)
        return acc + jnp.dot(vt_ref[kv, 0 : HD + 8, at : at + CHUNK], p, preferred_element_type=jnp.float32)

    def finish(g, kv, acc, top):
        total = acc[HD : HD + 1]
        o_buf[g, kv] = (acc[:HD] / total).T.astype(jnp.bfloat16).reshape(4, 4, 16, HD)
        lse = top + jnp.log2(total)
        l_buf[g, 2 * kv] = lse[:, :128]
        l_buf[g, 2 * kv + 1] = lse[:, 128:]

    low = jnp.full((8, ROWS), -jnp.inf, jnp.float32)
    zero = jnp.zeros((HD + 8, ROWS), jnp.float32)

    def attend(g, best):
        top = jnp.max(best, axis=0, keepdims=True) * SCALE
        q = head_q(g, 1)
        other, acc = low, zero
        for c in range(KEYS // CHUNK):
            other = scores(1, c, q, sb, other)
            acc = weigh(0, c, sa, top, acc)
        finish(g, 0, acc, top)
        top = jnp.max(other, axis=0, keepdims=True) * SCALE
        q = head_q(jnp.minimum(g + 1, GROUPS - 1), 0)
        best, acc = low, zero
        for c in range(KEYS // CHUNK):
            best = scores(0, c, q, sa, best)
            acc = weigh(1, c, sb, top, acc)
        finish(g, 1, acc, top)
        return best

    def place(g):
        odd = lax.rem(g, 2)
        a, b = x + odd * (z - x), z + odd * (x - z)

        def host(yy, aa, bb):
            return {"ctx": 16 * yy + (4 - 3 * odd) * aa + (1 + 3 * odd) * bb}

        return a, b, host

    def plane(g):
        a, b, host = place(g)
        for i in range(1, 8):
            q = lax.rem(4 * y + a + i, 8)
            yield q // 4, lax.rem(q, 4), host(q // 4, lax.rem(q, 4), b)

    def ring(g):
        a, b, host = place(g)
        for i in range(1, 4):
            bb = lax.rem(b + i, 4)
            yield bb, host(y, a, bb)

    def send_ring(g):
        a, b, _ = place(g)
        for bb, to in ring(g):
            remote(l_buf.at[g], l1.at[g, b], l1_send.at[g], l1_recv.at[g], to).start()
            for yy, at in QUARTERS:
                remote(
                    o_buf.at[g, yy, at, bb], r1.at[g, b, yy, at], o1_send.at[g], o1_recv.at[g], to
                ).start()
        pltpu.make_async_copy(l_buf.at[g], l1.at[g, b], l1_recv.at[g]).start()
        pltpu.make_async_copy(o_buf.at[g, :, :, b], r1.at[g, b], o1_recv.at[g]).start()

    def combine_ring(g):
        a, b, _ = place(g)
        drain(l1.at[g], l1_recv.at[g])
        lse = l1[g, :, :, 0, :]
        top = jnp.max(lse, axis=0)
        w = jnp.exp2(lse - top[None])
        total = jnp.sum(w, axis=0)
        w = (w / total[None]).reshape(16, 128)
        w1[...] = jnp.concatenate([w, jnp.zeros((112, 128), jnp.float32)], 0).T
        l2_buf[g, :, 0, :] = top + jnp.log2(total)
        drain(r1.at[g], o1_recv.at[g])
        for aa in range(4):
            ws = w1[pl.ds(pl.multiple_of(64 * (aa % 2) + 16 * b, 16), 16), :]
            for yy in range(2):
                acc = jnp.zeros((16, HD), jnp.float32)
                for src in range(4):
                    at = 4 * src + 2 * yy + aa // 2
                    acc = acc + ws[:, at : at + 1] * r1[g, src, yy, aa].astype(jnp.float32)
                s2[g, yy, aa] = acc.astype(jnp.bfloat16)
        mine = 4 * y + a
        for yy, aa, to in plane(g):
            remote(l2_buf.at[g, 2 * yy + aa // 2], l2.at[g, mine], l2_send.at[g], l2_recv.at[g], to).start()
            remote(s2.at[g, yy, aa], r2.at[g, mine], o2_send.at[g], o2_recv.at[g], to).start()
        pltpu.make_async_copy(l2_buf.at[g, 2 * y + a // 2], l2.at[g, mine], l2_recv.at[g]).start()
        pltpu.make_async_copy(s2.at[g, y, a], r2.at[g, mine], o2_recv.at[g]).start()

    def combine_plane(g):
        a, b, _ = place(g)
        drain(l2.at[g], l2_recv.at[g])
        lse = l2[g, :, 0, :]
        w = jnp.exp2(lse - jnp.max(lse, axis=0, keepdims=True))
        w = w / jnp.sum(w, axis=0, keepdims=True)
        w2[...] = jnp.concatenate([w, jnp.zeros((120, 128), jnp.float32)], 0).T
        drain(r2.at[g], o2_recv.at[g])
        ws = w2[pl.ds(pl.multiple_of(64 * lax.rem(a, 2) + 16 * b, 16), 16), :]
        acc = jnp.zeros((16, HD), jnp.float32)
        for src in range(8):
            acc = acc + ws[:, src : src + 1] * r2[g, src].astype(jnp.float32)
        at_buf[g, y, a, b] = acc.astype(jnp.bfloat16)
        own = at_buf.at[g, y, a, b]
        for _, _, to in plane(g):
            remote(own, own, a1_send.at[g], a1_recv.at[g], to).start()

    def gather_ring(g):
        a, b, _ = place(g)
        drain(r2.at[g, pl.ds(0, 7)], a1_recv.at[g])
        for _, to in ring(g):
            for yy, at in QUARTERS:
                own = at_buf.at[g, yy, at, b]
                remote(own, own, a2_send.at[g], a2_recv.at[g], to).start()

    def result(g, kv):
        return pltpu.make_async_copy(
            at_buf.at[g, kv], att_hbm.at[:, :, :, pl.ds(pl.multiple_of(kv * 1024 + g * HD, HD), HD)], out_sem.at[g]
        )

    def project(g):
        drain(r1.at[g, pl.ds(0, 3)], a2_recv.at[g])
        multiply(g)

    def multiply(g):
        for kv in range(2):
            result(g, kv).start()
            rows = pl.ds(pl.multiple_of(kv * 1024 + g * HD, HD), HD)
            part[...] += jnp.dot(
                at_buf[g, kv].reshape(ROWS, HD), w_ref[rows, :], preferred_element_type=jnp.float32
            )

    stages = (send_ring, combine_ring, combine_plane, gather_ring, project)

    def send_direct(g):
        j = g - STAGED
        for i in range(1, HOSTS):
            p = lax.rem(me + i, HOSTS)
            aa, bb = lax.rem(p // 4, 4), lax.rem(p, 4)
            remote(l_buf.at[g, p // 8], dl_recv.at[j, me], l1_send.at[g], l1_recv.at[g], {"ctx": p}).start()
            remote(o_buf.at[g, p // 16, aa, bb], d_recv.at[j, me], o1_send.at[g], o1_recv.at[g], {"ctx": p}).start()
        pltpu.make_async_copy(l_buf.at[g, me // 8], dl_recv.at[j, me], l1_recv.at[g]).start()
        pltpu.make_async_copy(o_buf.at[g, y, x, z], d_recv.at[j, me], o1_recv.at[g]).start()

    def combine_direct(g):
        j = g - STAGED
        drain(dl_recv.at[j], l1_recv.at[g])
        lse = dl_recv[j, :, 0, :]
        w = jnp.exp2(lse - jnp.max(lse, axis=0, keepdims=True))
        w = w / jnp.sum(w, axis=0, keepdims=True)
        w2[...] = jnp.concatenate([w, jnp.zeros((96, 128), jnp.float32)], 0).T
        drain(d_recv.at[j], o1_recv.at[g])
        ws = w2[pl.ds(pl.multiple_of(64 * lax.rem(x, 2) + 16 * z, 16), 16), :]
        acc = jnp.zeros((16, HD), jnp.float32)
        for src in range(HOSTS):
            acc = acc + ws[:, src : src + 1] * d_recv[j, src].astype(jnp.float32)
        at_buf[g, y, x, z] = acc.astype(jnp.bfloat16)
        own = at_buf.at[g, y, x, z]
        for i in range(1, HOSTS):
            remote(own, own, a1_send.at[g], a1_recv.at[g], {"ctx": lax.rem(me + i, HOSTS)}).start()

    def project_direct(g):
        drain(d_recv.at[g - STAGED, pl.ds(0, HOSTS - 1)], a1_recv.at[g])
        multiply(g)

    def exchange(g):
        for n in reversed(range(len(stages))):
            @pl.when((g >= AFTER[n]) & (g < STAGED + AFTER[n]))
            def _():
                stages[n](g - AFTER[n])

    part[...] = jnp.zeros_like(part)
    drain(q_ref.at[:, :, :, :, q_cols(0)], q1_recv.at[0])
    q = head_q(0, 0)
    best = low
    for c in range(KEYS // CHUNK):
        best = scores(0, c, q, sa, best)
    loads[2].wait()

    def step(g, best):
        for b in range(1, len(Q_BATCHES)):
            @pl.when(g == Q_BATCHES[b][0] - 1)
            def _():
                q_ready(b)

        best = attend(g, best)

        @pl.when(g >= STAGED)
        def _():
            send_direct(g)

        @pl.when(g >= STAGED + 2)
        def _():
            combine_direct(g - 2)

        exchange(g)
        return best

    lax.fori_loop(0, GROUPS, step, best)

    if STAGED <= GROUPS - 2:
        combine_direct(GROUPS - 2)
    for n in range(1, len(stages)):
        for g in range(STAGED):
            if GROUPS <= g + AFTER[n]:
                stages[n](g)
        if n == 1 and STAGED < GROUPS:
            combine_direct(GROUPS - 1)
    for g in range(STAGED, GROUPS):
        project_direct(g)

    hd_buf[...] = part[...].astype(jnp.bfloat16)
    for i in (1, 2, 3):
        to = lax.rem(hd + i, 4)
        for n in range(4):
            remote(
                hd_buf.at[pl.ds(pl.multiple_of(64 * to + 16 * n, 16), 16), :], hd_recv.at[i - 1, pl.ds(16 * n, 16)],
                h_send.at[i - 1], h_recv.at[i - 1], {"head": to},
            ).start()
    total = part[pl.ds(pl.multiple_of(64 * hd, 64), 64), :]
    for i in range(3):
        drain(hd_recv.at[i], h_recv.at[i])
        total = total + hd_recv[i].astype(jnp.float32)
    proj_ref[...] = total.astype(jnp.bfloat16)

    for b in range(len(Q_BATCHES)):
        n = Q_BATCHES[b][1] - Q_BATCHES[b][0]
        if b == 0:
            drain(o_buf.at[pl.ds(0, 2), 0, pl.ds(0, 3)], q1_send.at[b])
            drain(r2.at[pl.ds(0, 2), pl.ds(0, 7)], q1_send.at[b])
            drain(r2.at[pl.ds(0, 2), pl.ds(0, 6)], q1_send.at[b])
            drain(r2.at[pl.ds(0, 2), pl.ds(0, 6)], q1_send.at[b])
        else:
            drain(r2.at[pl.ds(0, n), pl.ds(0, 7)], q1_send.at[b])
            drain(q_ref.at[:, pl.ds(0, 3), :, :, q_cols(b)], q2_send.at[b])

    for g in range(STAGED):
        drain(r1.at[g, pl.ds(0, 3)], o1_send.at[g])
        drain(l1.at[g, pl.ds(0, 3)], l1_send.at[g])
        drain(r2.at[g, pl.ds(0, 7)], o2_send.at[g])
        drain(l2.at[g, pl.ds(0, 7)], l2_send.at[g])
        drain(r2.at[g, pl.ds(0, 7)], a1_send.at[g])
        drain(r1.at[g, pl.ds(0, 3)], a2_send.at[g])
    for j in range(GROUPS - STAGED):
        drain(d_recv.at[j, pl.ds(0, HOSTS - 1)], o1_send.at[STAGED + j])
        drain(dl_recv.at[j, pl.ds(0, HOSTS - 1)], l1_send.at[STAGED + j])
        drain(d_recv.at[j, pl.ds(0, HOSTS - 1)], a1_send.at[STAGED + j])
    for g in range(GROUPS):
        for kv in range(2):
            result(g, kv).wait()
    for i in range(3):
        drain(hd_recv.at[i], h_send.at[i])


def attention(qp, keys, values, lengths, w_out):
    vmem = pl.BlockSpec(memory_space=pltpu.VMEM)
    anywhere = pl.BlockSpec(memory_space=pl.ANY)
    bf, f32 = jnp.bfloat16, jnp.float32
    dma = pltpu.SemaphoreType.DMA
    nq, n = len(Q_BATCHES), GROUPS
    scratch = [
        ((2 * KEYS, HD), bf), ((2 * KEYS, HD), bf), ((2 * KEYS, HD), f32), ((2 * KEYS, HD), f32), ((HD, HD), bf),
        ((2048, 256), bf), ((2, KEYS, HD), bf), ((2, HD + 16, KEYS), bf), ((2, 4, 4, 16, 1024), bf),
        ((KEYS, ROWS), f32), ((KEYS, ROWS), f32),
        ((n, 2, 4, 4, 16, HD), bf), ((n, 4, 1, 128), f32), ((n, 4, 2, 4, 16, HD), bf), ((n, 4, 4, 1, 128), f32),
        ((n, 2, 4, 16, HD), bf), ((n, 4, 1, 128), f32), ((n, 8, 16, HD), bf), ((n, 8, 1, 128), f32),
        ((n - STAGED, HOSTS, 16, HD), bf), ((n - STAGED, HOSTS, 1, 128), f32),
        ((n, 2, 4, 4, 16, HD), bf), ((128, 128), f32), ((128, 128), f32),
        ((ROWS, 256), f32), ((ROWS, 256), bf), ((3, 64, 256), bf),
    ]
    sems = [3, n, nq, nq, nq, nq] + [n] * 12 + [3, 3]
    att, proj = pl.pallas_call(
        main_kernel,
        out_shape=(jax.ShapeDtypeStruct((4, 4, 16, 2048), bf), jax.ShapeDtypeStruct((64, 256), bf)),
        in_specs=[vmem, anywhere, anywhere, pl.BlockSpec(memory_space=pltpu.SMEM), anywhere],
        out_specs=(anywhere, vmem),
        scratch_shapes=[pltpu.VMEM(*s) for s in scratch] + [dma((k,)) for k in sems],
        compiler_params=pltpu.CompilerParams(
            collective_id=0, has_side_effects=True, vmem_limit_bytes=56 << 20
        ),
    )(qp, keys.reshape(2 * KEYS, HD), values.reshape(2 * KEYS, HD), lengths, w_out)
    return settle(att.reshape(ROWS, 2048), proj)


def settle_kernel(att_ref, proj_ref, att_out, proj_out):
    att_out[...] = att_ref[...]
    proj_out[...] = proj_ref[...]


def settle(att, proj):
    vmem = pl.BlockSpec(memory_space=pltpu.VMEM)
    return pl.pallas_call(
        settle_kernel,
        out_shape=(jax.ShapeDtypeStruct(att.shape, att.dtype), jax.ShapeDtypeStruct(proj.shape, proj.dtype)),
        in_specs=[vmem, vmem],
        out_specs=(vmem, vmem),
    )(att, proj)


def body(queries, keys, values, lengths, owner, w_out):
    qp = lax.switch(owner[0], [functools.partial(scatter, o) for o in range(HOSTS)], queries)
    return attention(qp, keys, values, lengths, w_out)


def solution(mesh):
    in_specs = (
        P("ctx", None, "head"),
        P("ctx", "head", None),
        P("ctx", "head", None),
        P("ctx"),
        P(),
        P("head", "ctx"),
    )
    out_specs = (P(None, "head"), P("head", "ctx"))
    return jax.shard_map(body, mesh=mesh, in_specs=in_specs, out_specs=out_specs, check_vma=False)
```

time: 103 us -> 86.1 us (0.84)
  Pallas kernels: 98.1 us -> 83.7 us
  local copies, waits for them, and re-layouts: 2.93 us -> 0 us
    pallas_call x1 -> x2, Pallas kernels: 85 us -> 68.3 us  [the longest x1 66.1 us: attention(): pl.pallas_call(main_kernel, out_shape=(jax.ShapeDtypeStruct((4, 4, 16, 20...]
    unnamed x4 -> x0, local copies, waits for them, and re-layouts: 2.93 us -> none
    pallas_call x1, Pallas kernels: 13.1 us -> 15.4 us  [scatter(): pl.pallas_call(functools.partial(scatter_kernel, owner), out_shape=jax.Sh...]
where the time goes in v2:
time: 86.1 us; the launch traced here: 85.9 us
  Pallas kernels  83.7 us (97%)
  between operations  1.94 us (2%)
    pallas_call x1, Pallas kernels, attention(): pl.pallas_call(main_kernel, out_shape=(jax.ShapeDtypeStruct((4, 4, 16, 20...  66.1 us
    pallas_call x1, Pallas kernels, scatter(): pl.pallas_call(functools.partial(scatter_kernel, owner), out_shape=jax.Sh...  15.4 us
    pallas_call x1, Pallas kernels, settle(): pl.pallas_call(settle_kernel, out_shape=(jax.ShapeDtypeStruct(att.shape,...  2.27 us

profile of v2, /device:TPU:1, one launch (start us, length us, event | category | flops | bytes accessed | tf_op | source)
XLA Modules:
  0.0 85.9 jit_solution(14580877109963107963)
XLA Ops:
  1.9 15.6 %conditional.1 = (bf16[16,1024]{1,0:T(8,128)(2,1)S(1)}) conditional(s32[]{:T(128)} %bitcast, bf16[1,256,2048]{2,1,0:T(8,128)(2,1)} %param.38, bf16[1,256,2048]{2,1,0:T(8,128)(2,1)} %param.38, bf16[1,256,2048]{2,1,0:T(8,128)(2,1)} %param.38, bf16[1,256,2048]{2,1,0:T(8,128)(2,1)} %param.38, ...), branch_computations={%region_0.0_spmd, %region_1.0_spmd, %region_2.0_spmd, %region_3.0_... | conditional | bytes 8 | solution.py:472
  2.0 15.4 %branch_26_fun.1 = bf16[16,1024]{1,0:T(8,128)(2,1)S(1)} custom-call(bf16[1,256,2048]{2,1,0:T(8,128)(2,1)} %q_ref.26), custom_call_target="tpu_custom_call" | custom-call | tf_op jit(solution)/shard_map/cond/branch_26_fun/pallas_call | solution.py:64
  17.6 66.1 %shard_map.173 = (bf16[4,4,16,2048]{3,2,1,0:T(8,128)(2,1)}, bf16[64,256]{1,0:T(8,128)(2,1)}) custom-call(bf16[16,1024]{1,0:T(8,128)(2,1)S(1)} %get-tuple-element.71.qp_ref, bf16[8192,128]{1,0:T(8,128)(2,1)} %bitcast.4, bf16[8192,128]{1,0:T(8,128)(2,1)} %bitcast.5, s32[1]{0:T(128)S(6)} %copy.40.len_ref, bf16[2048,256]{1,0:T(8,128)(2,1)} %w_hbm.1), custom_call_target="tpu_custom_call" | custom-call | tf_op jit(solution)/shard_map/pallas_call | solution.py:443
  83.7 2.3 %shard_map.174 = (bf16[256,2048]{1,0:T(8,128)(2,1)}, bf16[64,256]{1,0:T(8,128)(2,1)}) custom-call(bf16[256,2048]{1,0:T(8,128)(2,1)} %bitcast.6, bf16[64,256]{1,0:T(8,128)(2,1)} %get-tuple-element.70.proj_ref), custom_call_target="tpu_custom_call" | custom-call | tf_op jit(solution)/shard_map/pallas_call | solution.py:463

commit v3 on v2

--- a/solution.py
+++ b/solution.py
@@ -18,7 +18,10 @@
 SCALE = math.log2(math.e) / math.sqrt(HD)
 STAGED = 4
 AFTER = (0, 2, 4, 6, 8)
-QUARTERS = tuple((yy, pl.ds(aa, 2)) for yy in range(2) for aa in (0, 2))
+OTHERS = sorted(
+    ((dy, dx, dz) for dy in range(2) for dx in range(4) for dz in range(4) if (dy, dx, dz) != (0, 0, 0)),
+    key=lambda d: -(2 * d[0] + min(d[1], 4 - d[1]) + min(d[2], 4 - d[2])),
+)
 Q_BATCHES = ((0, 2, False), (2, 5, False), (5, 8, True))
 
 
@@ -49,8 +52,8 @@
             return q_ref.at[0, pl.ds(16 * (p % 16), 16), pl.ds(1024 * (p // 16), 1024)]
 
         copies = []
-        for step in range(1, HOSTS):
-            p = (owner + step) % HOSTS
+        for step, (dy, dx, dz) in enumerate(OTHERS, 1):
+            p = 16 * ((owner // 16 + dy) % 2) + 4 * ((owner // 4 + dx) % 4) + (owner + dz) % 4
             copies.append(remote(piece(p), out_ref, send.at[step], recv, {"ctx": p}))
             copies[-1].start()
         own = pltpu.make_async_copy(piece(owner), out_ref, send.at[0])
@@ -93,43 +96,6 @@
         pl.semaphore_signal(barrier, inc=1, device_id={"ctx": lax.rem(me + i, HOSTS)}, device_id_type=MESH)
     for i in range(1, 4):
         pl.semaphore_signal(barrier, inc=1, device_id={"head": lax.rem(hd + i, 4)}, device_id_type=MESH)
-    pl.semaphore_wait(barrier, HOSTS - 1 + 3)
-
-    def q_cols(b):
-        first, last, _ = Q_BATCHES[b]
-        return pl.ds(first * HD, (last - first) * HD)
-
-    def q_plane(b):
-        cols = q_cols(b)
-        return q_ref.at[:, x, :, :, cols] if Q_BATCHES[b][2] else q_ref.at[:, :, z, :, cols]
-
-    for b in range(len(Q_BATCHES)):
-        src, dst = qp_ref.at[:, q_cols(b)], q_ref.at[y, x, z, :, q_cols(b)]
-        if b == 0:
-            for i in range(1, HOSTS):
-                remote(src, dst, q1_send.at[b], q1_recv.at[b], {"ctx": lax.rem(me + i, HOSTS)}).start()
-        for i in range(1, 8) if b else ():
-            if Q_BATCHES[b][2]:
-                q = lax.rem(4 * y + z + i, 8)
-                to = 16 * (q // 4) + 4 * x + lax.rem(q, 4)
-            else:
-                q = lax.rem(4 * y + x + i, 8)
-                to = 16 * (q // 4) + 4 * lax.rem(q, 4) + z
-            remote(src, dst, q1_send.at[b], q1_recv.at[b], {"ctx": to}).start()
-        pltpu.make_async_copy(src, dst, q1_recv.at[b]).start()
-
-    def q_ring(b):
-        drain(q_plane(b), q1_recv.at[b])
-        for i in range(1, 4):
-            to = 16 * y + 4 * lax.rem(x + i, 4) + z if Q_BATCHES[b][2] else 16 * y + 4 * x + lax.rem(z + i, 4)
-            part_of = q_plane(b)
-            for yy, at in QUARTERS:
-                own = part_of.at[yy, at]
-                remote(own, own, q2_send.at[b], q2_recv.at[b], {"ctx": to}).start()
-
-    def q_ready(b):
-        drain(q_ref.at[:, pl.ds(0, 3), :, :, q_cols(b)], q2_recv.at[b])
-
     count = len_ref[0]
     loads[0].wait()
     for c in range(KEYS // 512):
@@ -140,6 +106,44 @@
             k_ref[kv, at : at + 512, :] = jnp.where(
                 row < count, k_wide[pl.ds(2 * at + kv, 512, stride=2), :], k_wide[kv : kv + 1, :]
             ).astype(jnp.bfloat16)
+    pl.semaphore_wait(barrier, HOSTS - 1 + 3)
+
+    def others():
+        for dy, dx, dz in OTHERS:
+            yield lax.rem(y + dy, 2), lax.rem(x + dx, 4), lax.rem(z + dz, 4)
+
+    def q_cols(b):
+        first, last, _ = Q_BATCHES[b]
+        return pl.ds(first * HD, (last - first) * HD)
+
+    def q_plane(b):
+        cols = q_cols(b)
+        return q_ref.at[:, x, :, :, cols] if Q_BATCHES[b][2] else q_ref.at[:, :, z, :, cols]
+
+    for b in range(len(Q_BATCHES)):
+        src, dst = qp_ref.at[:, q_cols(b)], q_ref.at[y, x, z, :, q_cols(b)]
+        if b == 0:
+            for yy, xx, zz in others():
+                remote(src, dst, q1_send.at[b], q1_recv.at[b], {"ctx": 16 * yy + 4 * xx + zz}).start()
+        for i in range(1, 8) if b else ():
+            if Q_BATCHES[b][2]:
+                q = lax.rem(4 * y + z + i, 8)
+                to = 16 * (q // 4) + 4 * x + lax.rem(q, 4)
+            else:
+                q = lax.rem(4 * y + x + i, 8)
+                to = 16 * (q // 4) + 4 * lax.rem(q, 4) + z
+            remote(src, dst, q1_send.at[b], q1_recv.at[b], {"ctx": to}).start()
+        pltpu.make_async_copy(src, dst, q1_recv.at[b]).start()
+
+    def q_ring(b):
+        drain(q_plane(b), q1_recv.at[b])
+        for i in range(1, 4):
+            to = 16 * y + 4 * lax.rem(x + i, 4) + z if Q_BATCHES[b][2] else 16 * y + 4 * x + lax.rem(z + i, 4)
+            remote(q_plane(b), q_plane(b), q2_send.at[b], q2_recv.at[b], {"ctx": to}).start()
+
+    def q_ready(b):
+        drain(q_ref.at[:, pl.ds(0, 3), :, :, q_cols(b)], q2_recv.at[b])
+
     loads[1].wait()
     eye[...] = jnp.where(
         lax.broadcasted_iota(jnp.int32, (HD, HD), 0) == lax.broadcasted_iota(jnp.int32, (HD, HD), 1), 1.0, 0.0
@@ -176,7 +180,7 @@
 
     def finish(g, kv, acc, top):
         total = acc[HD : HD + 1]
-        o_buf[g, kv] = (acc[:HD] / total).T.astype(jnp.bfloat16).reshape(4, 4, 16, HD)
+        o_buf[g, kv] = (acc[:HD] * (1.0 / total)).astype(jnp.bfloat16).T.reshape(4, 4, 16, HD)
         lse = top + jnp.log2(total)
         l_buf[g, 2 * kv] = lse[:, :128]
         l_buf[g, 2 * kv + 1] = lse[:, 128:]
@@ -226,10 +230,7 @@
         a, b, _ = place(g)
         for bb, to in ring(g):
             remote(l_buf.at[g], l1.at[g, b], l1_send.at[g], l1_recv.at[g], to).start()
-            for yy, at in QUARTERS:
-                remote(
-                    o_buf.at[g, yy, at, bb], r1.at[g, b, yy, at], o1_send.at[g], o1_recv.at[g], to
-                ).start()
+            remote(o_buf.at[g, :, :, bb], r1.at[g, b], o1_send.at[g], o1_recv.at[g], to).start()
         pltpu.make_async_copy(l_buf.at[g], l1.at[g, b], l1_recv.at[g]).start()
         pltpu.make_async_copy(o_buf.at[g, :, :, b], r1.at[g, b], o1_recv.at[g]).start()
 
@@ -280,9 +281,8 @@
         a, b, _ = place(g)
         drain(r2.at[g, pl.ds(0, 7)], a1_recv.at[g])
         for _, to in ring(g):
-            for yy, at in QUARTERS:
-                own = at_buf.at[g, yy, at, b]
-                remote(own, own, a2_send.at[g], a2_recv.at[g], to).start()
+            own = at_buf.at[g, :, :, b]
+            remote(own, own, a2_send.at[g], a2_recv.at[g], to).start()
 
     def result(g, kv):
         return pltpu.make_async_copy(
@@ -305,11 +305,10 @@
 
     def send_direct(g):
         j = g - STAGED
-        for i in range(1, HOSTS):
-            p = lax.rem(me + i, HOSTS)
-            aa, bb = lax.rem(p // 4, 4), lax.rem(p, 4)
-            remote(l_buf.at[g, p // 8], dl_recv.at[j, me], l1_send.at[g], l1_recv.at[g], {"ctx": p}).start()
-            remote(o_buf.at[g, p // 16, aa, bb], d_recv.at[j, me], o1_send.at[g], o1_recv.at[g], {"ctx": p}).start()
+        for yy, xx, zz in others():
+            p = {"ctx": 16 * yy + 4 * xx + zz}
+            remote(l_buf.at[g, 2 * yy + xx // 2], dl_recv.at[j, me], l1_send.at[g], l1_recv.at[g], p).start()
+            remote(o_buf.at[g, yy, xx, zz], d_recv.at[j, me], o1_send.at[g], o1_recv.at[g], p).start()
         pltpu.make_async_copy(l_buf.at[g, me // 8], dl_recv.at[j, me], l1_recv.at[g]).start()
         pltpu.make_async_copy(o_buf.at[g, y, x, z], d_recv.at[j, me], o1_recv.at[g]).start()
 
@@ -327,8 +326,8 @@
             acc = acc + ws[:, src : src + 1] * d_recv[j, src].astype(jnp.float32)
         at_buf[g, y, x, z] = acc.astype(jnp.bfloat16)
         own = at_buf.at[g, y, x, z]
-        for i in range(1, HOSTS):
-            remote(own, own, a1_send.at[g], a1_recv.at[g], {"ctx": lax.rem(me + i, HOSTS)}).start()
+        for yy, xx, zz in others():
+            remote(own, own, a1_send.at[g], a1_recv.at[g], {"ctx": 16 * yy + 4 * xx + zz}).start()
 
     def project_direct(g):
         drain(d_recv.at[g - STAGED, pl.ds(0, HOSTS - 1)], a1_recv.at[g])
@@ -459,12 +458,13 @@
 
 
 def settle(att, proj):
-    vmem = pl.BlockSpec(memory_space=pltpu.VMEM)
+    blocks = (pl.BlockSpec((128, 2048), lambda i: (i, 0)), pl.BlockSpec((32, 256), lambda i: (i, 0)))
     return pl.pallas_call(
         settle_kernel,
+        grid=(2,),
         out_shape=(jax.ShapeDtypeStruct(att.shape, att.dtype), jax.ShapeDtypeStruct(proj.shape, proj.dtype)),
-        in_specs=[vmem, vmem],
-        out_specs=(vmem, vmem),
+        in_specs=list(blocks),
+        out_specs=blocks,
     )(att, proj)
 
 

time: 86.1 us -> 83.9 us (0.974)
  Pallas kernels: 83.7 us -> 82.1 us
    pallas_call x1, Pallas kernels: 15.4 us -> 13.2 us  [scatter(): pl.pallas_call(functools.partial(scatter_kernel, owner), out_shape=jax.Sh...]
where the time goes in v3:
time: 83.9 us; the launch traced here: 84.3 us
  Pallas kernels  82.1 us (98%)
  between operations  1.94 us (2%)
    pallas_call x1, Pallas kernels, attention(): pl.pallas_call(main_kernel, out_shape=(jax.ShapeDtypeStruct((4, 4, 16, 20...  66.9 us
    pallas_call x1, Pallas kernels, scatter(): pl.pallas_call(functools.partial(scatter_kernel, owner), out_shape=jax.Sh...  13.2 us
    pallas_call x1, Pallas kernels, settle(): pl.pallas_call(settle_kernel, grid=(2,), out_shape=(jax.ShapeDtypeStruct(...  2.07 us

profile of v3, /device:TPU:1, one launch (start us, length us, event | category | flops | bytes accessed | tf_op | source)
XLA Modules:
  0.0 84.3 jit_solution(876191300398654345)
XLA Ops:
  1.9 13.4 %conditional.1 = (bf16[16,1024]{1,0:T(8,128)(2,1)S(1)}) conditional(s32[]{:T(128)} %bitcast, bf16[1,256,2048]{2,1,0:T(8,128)(2,1)} %param.38, bf16[1,256,2048]{2,1,0:T(8,128)(2,1)} %param.38, bf16[1,256,2048]{2,1,0:T(8,128)(2,1)} %param.38, bf16[1,256,2048]{2,1,0:T(8,128)(2,1)} %param.38, ...), branch_computations={%region_0.0_spmd, %region_1.0_spmd, %region_2.0_spmd, %region_3.0_... | conditional | bytes 8 | solution.py:472
  2.0 13.2 %branch_16_fun.1 = bf16[16,1024]{1,0:T(8,128)(2,1)S(1)} custom-call(bf16[1,256,2048]{2,1,0:T(8,128)(2,1)} %q_ref.16), custom_call_target="tpu_custom_call" | custom-call | tf_op jit(solution)/shard_map/cond/branch_16_fun/pallas_call | solution.py:67
  15.3 66.9 %shard_map.173 = (bf16[4,4,16,2048]{3,2,1,0:T(8,128)(2,1)}, bf16[64,256]{1,0:T(8,128)(2,1)}) custom-call(bf16[16,1024]{1,0:T(8,128)(2,1)S(1)} %get-tuple-element.71.qp_ref, bf16[8192,128]{1,0:T(8,128)(2,1)} %bitcast.4, bf16[8192,128]{1,0:T(8,128)(2,1)} %bitcast.5, s32[1]{0:T(128)S(6)} %copy.40.len_ref, bf16[2048,256]{1,0:T(8,128)(2,1)} %w_hbm.1), custom_call_target="tpu_custom_call" | custom-call | tf_op jit(solution)/shard_map/pallas_call | solution.py:442
  82.3 2.1 %shard_map.174 = (bf16[256,2048]{1,0:T(8,128)(2,1)}, bf16[64,256]{1,0:T(8,128)(2,1)}) custom-call(bf16[256,2048]{1,0:T(8,128)(2,1)} %bitcast.6, bf16[64,256]{1,0:T(8,128)(2,1)} %get-tuple-element.70.proj_ref), custom_call_target="tpu_custom_call" | custom-call | tf_op jit(solution)/shard_map/pallas_call | solution.py:462

commit v4 on v3

--- a/solution.py
+++ b/solution.py
@@ -17,6 +17,7 @@
 CHUNK = 1024
 SCALE = math.log2(math.e) / math.sqrt(HD)
 STAGED = 4
+DIRECT = ((4, 2), (6, 1), (7, 1))
 AFTER = (0, 2, 4, 6, 8)
 OTHERS = sorted(
     ((dy, dx, dz) for dy in range(2) for dx in range(4) for dz in range(4) if (dy, dx, dz) != (0, 0, 0)),
@@ -303,35 +304,40 @@
 
     stages = (send_ring, combine_ring, combine_plane, gather_ring, project)
 
-    def send_direct(g):
-        j = g - STAGED
+    def send_direct(g, n):
+        at, to = pl.ds(g, n), pl.ds(g - STAGED, n)
         for yy, xx, zz in others():
             p = {"ctx": 16 * yy + 4 * xx + zz}
-            remote(l_buf.at[g, 2 * yy + xx // 2], dl_recv.at[j, me], l1_send.at[g], l1_recv.at[g], p).start()
-            remote(o_buf.at[g, yy, xx, zz], d_recv.at[j, me], o1_send.at[g], o1_recv.at[g], p).start()
-        pltpu.make_async_copy(l_buf.at[g, me // 8], dl_recv.at[j, me], l1_recv.at[g]).start()
-        pltpu.make_async_copy(o_buf.at[g, y, x, z], d_recv.at[j, me], o1_recv.at[g]).start()
-
-    def combine_direct(g):
-        j = g - STAGED
-        drain(dl_recv.at[j], l1_recv.at[g])
-        lse = dl_recv[j, :, 0, :]
-        w = jnp.exp2(lse - jnp.max(lse, axis=0, keepdims=True))
-        w = w / jnp.sum(w, axis=0, keepdims=True)
-        w2[...] = jnp.concatenate([w, jnp.zeros((96, 128), jnp.float32)], 0).T
-        drain(d_recv.at[j], o1_recv.at[g])
-        ws = w2[pl.ds(pl.multiple_of(64 * lax.rem(x, 2) + 16 * z, 16), 16), :]
-        acc = jnp.zeros((16, HD), jnp.float32)
-        for src in range(HOSTS):
-            acc = acc + ws[:, src : src + 1] * d_recv[j, src].astype(jnp.float32)
-        at_buf[g, y, x, z] = acc.astype(jnp.bfloat16)
-        own = at_buf.at[g, y, x, z]
+            remote(
+                l_buf.at[at, 2 * yy + xx // 2], dl_recv.at[to, me], l1_send.at[g], l1_recv.at[g], p
+            ).start()
+            remote(o_buf.at[at, yy, xx, zz], d_recv.at[to, me], o1_send.at[g], o1_recv.at[g], p).start()
+        pltpu.make_async_copy(l_buf.at[at, me // 8], dl_recv.at[to, me], l1_recv.at[g]).start()
+        pltpu.make_async_copy(o_buf.at[at, y, x, z], d_recv.at[to, me], o1_recv.at[g]).start()
+
+    def combine_direct(g, n):
+        to = pl.ds(g - STAGED, n)
+        drain(dl_recv.at[to], l1_recv.at[g])
+        drain(d_recv.at[to], o1_recv.at[g])
+        for k in range(n):
+            j = g - STAGED + k
+            lse = dl_recv[j, :, 0, :]
+            w = jnp.exp2(lse - jnp.max(lse, axis=0, keepdims=True))
+            w = w / jnp.sum(w, axis=0, keepdims=True)
+            w2[...] = jnp.concatenate([w, jnp.zeros((96, 128), jnp.float32)], 0).T
+            ws = w2[pl.ds(pl.multiple_of(64 * lax.rem(x, 2) + 16 * z, 16), 16), :]
+            acc = jnp.zeros((16, HD), jnp.float32)
+            for src in range(HOSTS):
+                acc = acc + ws[:, src : src + 1] * d_recv[j, src].astype(jnp.float32)
+            at_buf[g + k, y, x, z] = acc.astype(jnp.bfloat16)
+        own = at_buf.at[pl.ds(g, n), y, x, z]
         for yy, xx, zz in others():
             remote(own, own, a1_send.at[g], a1_recv.at[g], {"ctx": 16 * yy + 4 * xx + zz}).start()
 
-    def project_direct(g):
-        drain(d_recv.at[g - STAGED, pl.ds(0, HOSTS - 1)], a1_recv.at[g])
-        multiply(g)
+    def project_direct(g, n):
+        drain(d_recv.at[pl.ds(g - STAGED, n), pl.ds(0, HOSTS - 1)], a1_recv.at[g])
+        for k in range(n):
+            multiply(g + k)
 
     def exchange(g):
         for n in reversed(range(len(stages))):
@@ -355,29 +361,29 @@
 
         best = attend(g, best)
 
-        @pl.when(g >= STAGED)
+        for first, n in DIRECT:
+            @pl.when(g == first + n - 1)
+            def _():
+                send_direct(first, n)
+
+        @pl.when(g == GROUPS - 1)
         def _():
-            send_direct(g)
-
-        @pl.when(g >= STAGED + 2)
-        def _():
-            combine_direct(g - 2)
+            combine_direct(*DIRECT[0])
 
         exchange(g)
         return best
 
     lax.fori_loop(0, GROUPS, step, best)
 
-    if STAGED <= GROUPS - 2:
-        combine_direct(GROUPS - 2)
+    combine_direct(*DIRECT[1])
     for n in range(1, len(stages)):
         for g in range(STAGED):
             if GROUPS <= g + AFTER[n]:
                 stages[n](g)
-        if n == 1 and STAGED < GROUPS:
-            combine_direct(GROUPS - 1)
-    for g in range(STAGED, GROUPS):
-        project_direct(g)
+        if n == 1:
+            combine_direct(*DIRECT[2])
+    for first, n in DIRECT:
+        project_direct(first, n)
 
     hd_buf[...] = part[...].astype(jnp.bfloat16)
     for i in (1, 2, 3):
@@ -411,10 +417,11 @@
         drain(l2.at[g, pl.ds(0, 7)], l2_send.at[g])
         drain(r2.at[g, pl.ds(0, 7)], a1_send.at[g])
         drain(r1.at[g, pl.ds(0, 3)], a2_send.at[g])
-    for j in range(GROUPS - STAGED):
-        drain(d_recv.at[j, pl.ds(0, HOSTS - 1)], o1_send.at[STAGED + j])
-        drain(dl_recv.at[j, pl.ds(0, HOSTS - 1)], l1_send.at[STAGED + j])
-        drain(d_recv.at[j, pl.ds(0, HOSTS - 1)], a1_send.at[STAGED + j])
+    for first, n in DIRECT:
+        sent = pl.ds(first - STAGED, n), pl.ds(0, HOSTS - 1)
+        drain(d_recv.at[sent], o1_send.at[first])
+        drain(dl_recv.at[sent], l1_send.at[first])
+        drain(d_recv.at[sent], a1_send.at[first])
     for g in range(GROUPS):
         for kv in range(2):
             result(g, kv).wait()

time: 83.9 us -> 83.5 us (level)
    pallas_call x1, Pallas kernels: 66.9 us -> 58.8 us  [attention(): pl.pallas_call(main_kernel, out_shape=(jax.ShapeDtypeStruct((4, 4, 16, 20...]
    pallas_call x1, Pallas kernels: 13.2 us -> 21 us  [scatter(): pl.pallas_call(functools.partial(scatter_kernel, owner), out_shape=jax.Sh...]
where the time goes in v4:
time: 83.5 us; the launch traced here: 84 us
  Pallas kernels  81.8 us (98%)
  between operations  1.94 us (2%)
    pallas_call x1, Pallas kernels, attention(): pl.pallas_call(main_kernel, out_shape=(jax.ShapeDtypeStruct((4, 4, 16, 20...  58.8 us
    pallas_call x1, Pallas kernels, scatter(): pl.pallas_call(functools.partial(scatter_kernel, owner), out_shape=jax.Sh...  21 us
    pallas_call x1, Pallas kernels, settle(): pl.pallas_call(settle_kernel, grid=(2,), out_shape=(jax.ShapeDtypeStruct(...  2.07 us

profile of v4, /device:TPU:1, one launch (start us, length us, event | category | flops | bytes accessed | tf_op | source)
XLA Modules:
  0.0 84.0 jit_solution(9865241779618683505)
XLA Ops:
  1.9 21.2 %conditional.1 = (bf16[16,1024]{1,0:T(8,128)(2,1)S(1)}) conditional(s32[]{:T(128)} %bitcast, bf16[1,256,2048]{2,1,0:T(8,128)(2,1)} %param.38, bf16[1,256,2048]{2,1,0:T(8,128)(2,1)} %param.38, bf16[1,256,2048]{2,1,0:T(8,128)(2,1)} %param.38, bf16[1,256,2048]{2,1,0:T(8,128)(2,1)} %param.38, ...), branch_computations={%region_0.0_spmd, %region_1.0_spmd, %region_2.0_spmd, %region_3.0_... | conditional | bytes 8 | solution.py:479
  2.0 21.0 %branch_0_fun.1 = bf16[16,1024]{1,0:T(8,128)(2,1)S(1)} custom-call(bf16[1,256,2048]{2,1,0:T(8,128)(2,1)} %q_ref), custom_call_target="tpu_custom_call" | custom-call | tf_op jit(solution)/shard_map/cond/branch_0_fun/pallas_call | solution.py:68
  23.2 58.8 %shard_map.173 = (bf16[4,4,16,2048]{3,2,1,0:T(8,128)(2,1)}, bf16[64,256]{1,0:T(8,128)(2,1)}) custom-call(bf16[16,1024]{1,0:T(8,128)(2,1)S(1)} %get-tuple-element.71.qp_ref, bf16[8192,128]{1,0:T(8,128)(2,1)} %bitcast.4, bf16[8192,128]{1,0:T(8,128)(2,1)} %bitcast.5, s32[1]{0:T(128)S(6)} %copy.40.len_ref, bf16[2048,256]{1,0:T(8,128)(2,1)} %w_hbm.1), custom_call_target="tpu_custom_call" | custom-call | tf_op jit(solution)/shard_map/pallas_call | solution.py:449
  82.0 2.1 %shard_map.174 = (bf16[256,2048]{1,0:T(8,128)(2,1)}, bf16[64,256]{1,0:T(8,128)(2,1)}) custom-call(bf16[256,2048]{1,0:T(8,128)(2,1)} %bitcast.6, bf16[64,256]{1,0:T(8,128)(2,1)} %get-tuple-element.70.proj_ref), custom_call_target="tpu_custom_call" | custom-call | tf_op jit(solution)/shard_map/pallas_call | solution.py:469
